TPU v7x, 512 devices: a whole 4x8x8 slice. The times are simulated.
512 devices in a mesh: row: 16 (over y_lo, x, core), col: 32 (over y_hi, z).
Axes of the slice: x: 4, y: 8 (y_hi: 4, y_lo: 2; y = y_hi * 2 + y_lo), z: 8, core: 2. Of those that a mesh axis runs over, the one named last changes fastest.
Arguments:
- out_left: bfloat16 [512, 512, 128], P('row', 'col'), may hold values from -6 to 6
- out_right: bfloat16 [512, 512, 128], P('col', 'row'), may hold values from -6 to 6
- in_left: bfloat16 [512, 512, 128], P('col', 'row'), may hold values from -6 to 6
- in_right: bfloat16 [512, 512, 128], P('row', 'col'), may hold values from -6 to 6
Outputs:
- outgoing: bfloat16 [512, 512, 128], P('row', 'col')
- incoming: bfloat16 [512, 512, 128], P('row', 'col')
All inputs are finite; a program needn't handle non-finite values.
Results may differ from a plain program's by a relative error of at most 0.001.
Values may be sent and summed in bfloat16 or wider, within the bound.
No kernel may reach another device: no remote copies, remote signals or barrier semaphores. Data moves between devices by JAX's collectives and lax.ppermute only.
A program may use at most 128 MiB of HBM per device.

v0:
```python
import math

import jax
import jax.numpy as jnp
from jax import lax
from jax.sharding import PartitionSpec as P


def body(out_left, out_right, in_left, in_right):
    total = out_left.shape[1] * lax.axis_size("col")
    factor = 1.0 / math.sqrt(total)
    right_out = lax.all_gather(out_right, "row", axis=1, tiled=True)
    right_in = lax.all_gather(in_right, "row", axis=0, tiled=True)
    matching = right_out
    sum_out = jnp.einsum(
        "ikc,jkc->ijc",
        lax.all_gather(out_left, "col", axis=1, tiled=True),
        matching,
        preferred_element_type=jnp.float32,
    )
    matching = right_in
    sum_in = jnp.einsum(
        "kic,kjc->ijc",
        lax.all_gather(in_left, "col", axis=0, tiled=True),
        matching,
        preferred_element_type=jnp.float32,
    )
    return ((sum_out * factor).astype(jnp.bfloat16), (sum_in * factor).astype(jnp.bfloat16))


def solution(mesh):
    in_specs = (
        P("row", "col", None),
        P("col", "row", None),
        P("col", "row", None),
        P("row", "col", None),
    )
    out_specs = (P("row", "col", None), P("row", "col", None))
    return jax.shard_map(body, mesh=mesh, in_specs=in_specs, out_specs=out_specs, check_vma=False)
```

profile of v0, /device:TPU:12, one launch (start us, length us, event | category | flops | bytes accessed | tf_op | source)
XLA Modules:
  0.0 568.3 jit_solution(16351118561812111723)
XLA Ops:
  7.2 0.0 all-gather.5.cloned.1.call-start
  7.2 1.6 copy.12
  8.8 0.0 all-gather.5.cloned.1.call-update
  8.8 0.0 all-gather.9.cloned.1.call-start
  8.9 0.7 all-gather.9.cloned.1.call-update
  9.6 0.0 all-gather.7.cloned.1.call-start
  9.6 2.2 copy.13
  11.8 0.0 all-gather.7.cloned.1.call-update
  11.8 0.0 all-gather.11.cloned.1.call-start
  11.9 2.1 copy.15
  14.0 0.0 all-gather.11.cloned.1.call-update
  14.0 39.2 %all-gather.5.cloned.1.call-done = bf16[16,512,128]{2,0,1:T(8,128)(2,1)} async-done(((bf16[16,32,128]{2,0,1:T(8,128)(2,1)}), bf16[16,512,128]{2,0,1:T(8,128)(2,1)}) %all-gather.5.cloned.1.call-update) | async-done | bytes 2097168 | tf_op jit(solution)/shard_map/all_gather | solution.py:12
  53.2 4.9 copy.14
  58.1 36.5 %all-gather.9.cloned.1.call-done = bf16[512,16,128]{2,1,0:T(8,128)(2,1)} async-done(((bf16[32,16,128]{2,1,0:T(8,128)(2,1)}), bf16[512,16,128]{2,1,0:T(8,128)(2,1)}) %all-gather.9.cloned.1.call-update) | async-done | bytes 2097168 | tf_op jit(solution)/shard_map/all_gather | solution.py:13
  94.6 3.9 copy.16
  98.5 228.6 %all-gather.7.cloned.1.call-done = bf16[32,512,128]{0,1,2:T(8,128)(2,1)} async-done(((bf16[32,16,128]{0,1,2:T(8,128)(2,1)}), bf16[32,512,128]{0,1,2:T(8,128)(2,1)}) %all-gather.7.cloned.1.call-update) | async-done | bytes 4194320 | tf_op jit(solution)/shard_map/all_gather | solution.py:17
  327.1 8.7 %fusion.3 = bf16[32,16,128]{0,1,2:T(8,128)(2,1)S(1)} fusion(bf16[16,512,128]{1,0,2:T(8,128)(2,1)} %copy.14, bf16[32,512,128]{0,1,2:T(8,128)(2,1)} %all-gather.7.cloned.1.call-done), kind=kOutput, calls=%fused_computation.5 | convolution fusion | flops 67239936 | bytes 6422528 | tf_op jit(solution)/shard_map/ikc,jkc->ijc/dot_general | solution.py:15
  335.8 1.2 copy.17
  337.0 216.4 %all-gather.11.cloned.1.call-done = bf16[512,32,128]{1,0,2:T(8,128)(2,1)} async-done(((bf16[16,32,128]{1,0,2:T(8,128)(2,1)}), bf16[512,32,128]{1,0,2:T(8,128)(2,1)}) %all-gather.11.cloned.1.call-update) | async-done | bytes 4194320 | tf_op jit(solution)/shard_map/all_gather | solution.py:24
  553.4 7.2 %fusion.2 = bf16[32,16,128]{0,1,2:T(8,128)(2,1)S(1)} fusion(bf16[512,16,128]{0,1,2:T(8,128)(2,1)S(1)} %copy.16, bf16[512,32,128]{1,0,2:T(8,128)(2,1)} %all-gather.11.cloned.1.call-done), kind=kOutput, calls=%fused_computation.4 | convolution fusion | flops 67239936 | bytes 6422528 | tf_op jit(solution)/shard_map/kic,kjc->ijc/dot_general | solution.py:22
  560.6 1.2 copy.18
Async XLA Ops:
  7.2 46.1 %all-gather.5.cloned.1.call-start = ((), (), s32[]{:S(2)}) async-start(), calls=%async_computation | async-start | bytes 2228224 | tf_op jit(solution)/shard_map/all_gather | solution.py:12
  8.8 85.8 %all-gather.9.cloned.1.call-start = ((), (), s32[]{:S(2)}) async-start(), calls=%async_computation.2 | async-start | bytes 2228224 | tf_op jit(solution)/shard_map/all_gather | solution.py:13
  9.6 317.5 %all-gather.7.cloned.1.call-start = ((), (), s32[]{:S(2)}) async-start(), calls=%async_computation.1 | async-start | bytes 17301504 | tf_op jit(solution)/shard_map/all_gather | solution.py:17
  11.8 541.5 %all-gather.11.cloned.1.call-start = ((), (), s32[]{:S(2)}) async-start(), calls=%async_computation.3 | async-start | bytes 17301504 | tf_op jit(solution)/shard_map/all_gather | solution.py:24
Sparse Core Ops, SparseCore 0:
  10.7 42.4 all-gather.4
  55.4 39.1 all-gather.8
  97.7 229.3 all-gather.6
  330.0 223.3 all-gather.10
where the time goes:
time: 569 us; the launch traced here: 568 us
  waiting for transfers between devices  521 us (92%)
  local copies, waits for them, and re-layouts  17 us (3%)
  matrix products  15.9 us (3%)
  between operations  13.8 us (2%)
    all_gather x1, waiting for transfers between devices, body(): lax.all_gather(out_left, 'col', axis=1, tiled=True)  229 us
    all_gather x1, waiting for transfers between devices, body(): lax.all_gather(in_left, 'col', axis=0, tiled=True)  216 us
    all_gather x1, waiting for transfers between devices, body(): right_out = lax.all_gather(out_right, 'row', axis=1, tiled=True)  39.2 us
    all_gather x1, waiting for transfers between devices, body(): right_in = lax.all_gather(in_right, 'row', axis=0, tiled=True)  36.5 us
  transfers between devices with their start and end apart: 4, of which 4 were waited for; matrix products, arithmetic and copies ran while one was open for 4% of the time, Pallas kernels for 0%

commit v1 on v0

v1 whole, which is shorter than its diff:
```python
import math

import jax
import jax.numpy as jnp
from jax import lax
from jax.sharding import Mesh, PartitionSpec as P

ROW = ("y_lo", "x", "core")
COL = ("y_hi", "z")
CHIPS = ("y_lo", "x", "y_hi", "z")


def body(out_left, out_right, in_left, in_right):
    left = jnp.stack([out_left, in_left.transpose(1, 0, 2)])
    right = jnp.stack([out_right.transpose(1, 0, 2), in_right])
    both = jnp.stack([left, right])
    sent = both.transpose(1, 4, 0, 2, 3).reshape(256, 8, 128)
    got = lax.all_to_all(sent, CHIPS, 0, 0, tiled=True)
    got = got.reshape(8, 32, 2, 32, 16).transpose(2, 0, 3, 1, 4).reshape(2, 256, 512)
    other = lax.all_gather(got[1].reshape(8, 32, 512), "core", axis=1, tiled=False)
    total = jnp.dot(got[0], other.reshape(512, 512), preferred_element_type=jnp.float32)
    factor = 1.0 / math.sqrt(512)
    result = (total * factor).astype(jnp.bfloat16)
    back = result.reshape(8, 32, 32, 16).transpose(0, 2, 1, 3).reshape(256, 4, 128)
    mine = lax.all_to_all(back, CHIPS, 0, 0, tiled=True)
    mine = mine.reshape(2, 128, 512).transpose(0, 2, 1).reshape(2, 32, 16, 128)
    return mine[0], mine[1]


def solution(mesh):
    fine = Mesh(mesh.devices.reshape(2, 4, 2, 4, 8), ROW + COL)
    in_specs = (P(ROW, COL, None), P(COL, ROW, None), P(COL, ROW, None), P(ROW, COL, None))
    out_specs = (P(ROW, COL, None), P(ROW, COL, None))
    return jax.shard_map(body, mesh=fine, in_specs=in_specs, out_specs=out_specs, check_vma=False)
```

time: 569 us -> 88.7 us (0.16)
  the two profiles are of different devices: /device:TPU:12 before, /device:TPU:8 now
where the time goes in v1:
time: 88.7 us; the launch traced here: 88.4 us
  blocking collectives  69.5 us (78%)
  local copies, waits for them, and re-layouts  16.7 us (19%)
  other arithmetic  1.07 us (1%)
    all_to_all x1, blocking collectives, body(): got = lax.all_to_all(sent, CHIPS, 0, 0, tiled=True)  42.8 us
    all_to_all x1, blocking collectives, body(): mine = lax.all_to_all(back, CHIPS, 0, 0, tiled=True)  24.5 us
    slice x2, local copies, waits for them, and re-layouts, body(): got[1].reshape(8, 32, 512)  3.82 us
    transpose x1, local copies, waits for them, and re-layouts, body(): result.reshape(8, 32, 32, 16).transpose(0, 2, 1, 3).reshape(256, 4, 128)  2.21 us
    slice x1, local copies, waits for them, and re-layouts, body(): got[0]  2.21 us
    all_gather x1, blocking collectives, body(): lax.all_gather(got[1].reshape(8, 32, 512), 'core', axis=1, tiled=False)  2.18 us
    unnamed x2, local copies, waits for them, and re-layouts  1.92 us

profile of v1, /device:TPU:8, one launch (start us, length us, event | category | flops | bytes accessed | tf_op | source)
XLA Modules:
  0.0 88.4 jit_solution(3419521896885585599)
XLA Ops:
  0.6 1.0 %copy.45 = bf16[16,32,128]{2,0,1:T(8,128)(2,1)S(1)} copy(bf16[16,32,128]{2,1,0:T(8,128)(2,1)} %param.5) | data formatting | bytes 262144 | tf_op args[1]
  1.6 1.0 %copy.46 = bf16[16,32,128]{2,0,1:T(8,128)(2,1)S(1)} copy(bf16[16,32,128]{2,1,0:T(8,128)(2,1)} %param.6) | data formatting | bytes 262144 | tf_op args[2]
  2.6 1.0 %maximum_bitcast_fusion.1 = (bf16[1,2,32,16,128]{4,3,2,1,0:T(8,128)(2,1)S(1)}, bf16[1,2,32,16,128]{4,3,2,1,0:T(8,128)(2,1)S(1)}) fusion(bf16[1,32,16,128]{3,2,1,0:T(8,128)(2,1)S(1)} %bitcast.47, bf16[1,32,16,128]{3,2,1,0:T(8,128)(2,1)} %bitcast.50, bf16[1,32,16,128]{3,2,1,0:T(8,128)(2,1)} %bitcast.51, bf16[1,32,16,128]{3,2,1,0:T(8,128)(2,1)S(1)} %bitcast.46), kind=kLoop, calls=%fused_computation.3 | loop fusion | flops 262144 | bytes 1048576 | tf_op jit(solution)/shard_map/stack | solution.py:16
  3.6 0.5 copy.31
  4.2 0.3 reshape.32
  4.5 0.3 copy.32
  4.8 42.8 %all_to_all.10 = bf16[256,8,128]{2,1,0:T(8,128)(2,1)S(1)} all-to-all(bf16[256,8,128]{2,1,0:T(8,128)(2,1)S(1)} %copy.32), channel_id=1, replica_groups=mesh['y_lo'=2,'x'=4,'core'=2,'y_hi'=4,'z'=8] {'y_lo','x','y_hi','z'}, dimensions={0} | all-to-all | bytes 1048576 | tf_op jit(solution)/shard_map/all_to_all | solution.py:18
  47.6 0.3 copy.33
  48.0 0.9 %reshape.33 = bf16[8,32,2,32,16]{1,0,4,3,2:T(8,128)(2,1)S(1)} reshape(bf16[256,8,128]{0,2,1:T(8,128)(2,1)S(1)} %copy.33) | data formatting | bytes 1048576 | tf_op jit(solution)/shard_map/reshape | solution.py:19
  48.9 1.2 %fusion.1 = (bf16[1,8,32,32,16]{3,1,4,2,0:T(8,128)(2,1)}, bf16[1,8,32,32,16]{3,1,4,2,0:T(8,128)(2,1)S(1)}) fusion(bf16[2,8,32,32,16]{3,1,4,2,0:T(8,128)(2,1)S(1)} %bitcast.41), kind=kLoop, calls=%fused_computation.7 | loop fusion | bytes 1048576 | tf_op jit(solution)/shard_map/slice | solution.py:20
  50.1 2.7 %copy.35 = bf16[1,8,32,32,16]{2,4,3,1,0:T(8,128)(2,1)S(1)} copy(bf16[1,8,32,32,16]{3,1,4,2,0:T(8,128)(2,1)} %get-tuple-element.4) | data formatting | bytes 524288 | tf_op jit(solution)/shard_map/slice | solution.py:20
  52.7 0.3 copy.36
  53.0 2.2 %all_gather.3 = bf16[8,2,32,512]{3,2,0,1:T(8,128)(2,1)S(1)} all-gather(bf16[8,1,32,512]{3,2,0,1:T(8,128)(2,1)S(1)} %copy.36), channel_id=1, replica_groups=mesh['y_lo'=2,'x'=4,'core'=2,'y_hi'=4,'z'=8] {'core'}, dimensions={1}, use_global_device_ids=true | all-gather | bytes 786432 | tf_op jit(solution)/shard_map/all_gather | solution.py:20
  55.3 2.2 %copy.34 = bf16[1,8,32,32,16]{2,1,4,3,0:T(8,128)(2,1)S(1)} copy(bf16[1,8,32,32,16]{3,1,4,2,0:T(8,128)(2,1)S(1)} %get-tuple-element.5) | data formatting | bytes 524288 | tf_op jit(solution)/shard_map/slice | solution.py:21
  57.5 0.7 squeeze.9
  58.2 0.3 fusion
  58.5 0.1 copy.38
  58.7 0.4 reshape.35
  59.1 2.2 %copy.39 = bf16[8,32,32,16]{1,0,3,2:T(8,128)(2,1)S(1)} copy(bf16[8,32,32,16]{2,0,3,1:T(8,128)(2,1)S(1)} %bitcast.43) | data formatting | bytes 524288 | tf_op jit(solution)/shard_map/transpose | solution.py:24
  61.3 0.7 reshape.36
  62.0 0.2 copy.40
  62.2 24.5 %all_to_all.11 = bf16[256,4,128]{2,1,0:T(4,128)(2,1)S(1)} all-to-all(bf16[256,4,128]{2,1,0:T(4,128)(2,1)S(1)} %copy.40), channel_id=1, replica_groups=mesh['y_lo'=2,'x'=4,'core'=2,'y_hi'=4,'z'=8] {'y_lo','x','y_hi','z'}, dimensions={0} | all-to-all | bytes 524288 | tf_op jit(solution)/shard_map/all_to_all | solution.py:25
  86.9 0.8 copy.42
  87.6 0.8 copy.41
  (4 shorter events, 0.2 us)

commit v2 on v1

v2 whole, which is shorter than its diff:
```python
import math

import jax
import jax.numpy as jnp
from jax import lax
from jax.experimental import pallas as pl
from jax.experimental.pallas import tpu as pltpu
from jax.sharding import Mesh, PartitionSpec as P

ROW = ("y_lo", "x", "core")
COL = ("y_hi", "z")
CHIPS = ("y_lo", "x", "y_hi", "z")
FACTOR = 1.0 / math.sqrt(512)
VMEM_BYTES = 32 * 1024 * 1024


def call(kernel, shape, scratch, *args):
    return pl.pallas_call(
        kernel,
        out_shape=shape,
        in_specs=[pl.BlockSpec(memory_space=pltpu.VMEM)] * len(args),
        out_specs=jax.tree.map(lambda _: pl.BlockSpec(memory_space=pltpu.VMEM), shape),
        scratch_shapes=[pltpu.VMEM(s, jnp.float32) for s in scratch],
        compiler_params=pltpu.CompilerParams(vmem_limit_bytes=VMEM_BYTES),
    )(*args)


def flip(block):
    n = block.shape[1]
    eye = lax.broadcasted_iota(jnp.int32, (n, n), 0) == lax.broadcasted_iota(jnp.int32, (n, n), 1)
    eye = eye.astype(jnp.float32).astype(jnp.bfloat16)
    return lax.dot_general(eye, block, (((1,), (1,)), ((), ())), preferred_element_type=jnp.float32)


def swap(v):
    lane = lax.broadcasted_iota(jnp.int32, v[0].shape, 1)
    even, low = (lane // 32) % 2 == 0, lane < 64

    def pair(x, y, first, by):
        return (
            jnp.where(first, x, pltpu.roll(y, by, 1)),
            jnp.where(first, pltpu.roll(x, 128 - by, 1), y),
        )

    a0, a1 = pair(v[0], v[1], even, 32)
    a2, a3 = pair(v[2], v[3], even, 32)
    w0, w2 = pair(a0, a2, low, 64)
    w1, w3 = pair(a1, a3, low, 64)
    return w0, w1, w2, w3


def pack_kernel(out_left, out_right, in_left, in_right, sent, rows, held):
    for product, side, ref, a_first in (
        (0, 0, out_left, True),
        (0, 1, out_right, False),
        (1, 0, in_left, False),
        (1, 1, in_right, True),
    ):
        if a_first:
            rows[...] = ref[...].reshape(512, 128).astype(jnp.float32)
            block = jnp.concatenate([rows[pl.ds(b, 32, stride=16), :] for b in range(16)])
            block = block.astype(jnp.bfloat16)
        else:
            block = ref[...].reshape(512, 128)
        turned = flip(block)
        for q in range(4):
            held[pl.ds(product * 1024 + side * 4 + q, 128, stride=8), :] = turned[:, q * 128 : (q + 1) * 128]
    sent[...] = held[...].astype(jnp.bfloat16).reshape(256, 8, 128)


def pack(out_left, out_right, in_left, in_right):
    return call(
        pack_kernel,
        jax.ShapeDtypeStruct((256, 8, 128), jnp.bfloat16),
        [(512, 128), (2048, 128)],
        out_left, out_right, in_left, in_right,
    )


def wide(ref, parts):
    return jnp.concatenate(
        [ref[p * 512 : (p + 1) * 512, :].astype(jnp.bfloat16) for p in range(parts)], axis=1
    )


def multiply_kernel(got, right, back, got_f, right_f, lhs, rhs, out):
    got_f[...] = got[...].reshape(2048, 128).astype(jnp.float32)
    right_f[...] = right[...].astype(jnp.float32).reshape(2048, 128)
    for q in range(4):
        for half in range(2):
            v = [got_f[pl.ds((half * 4 + r) * 256 + q, 32, stride=8), :] for r in range(4)]
            for g, w in enumerate(swap(v)):
                lhs[pl.ds(half * 512 + q * 4 + g, 32, stride=16), :] = w
        for part in range(4):
            v = [
                right_f[pl.ds((r % 2) * 1024 + (part * 2 + r // 2) * 128 + q, 32, stride=4), :]
                for r in range(4)
            ]
            for g, w in enumerate(swap(v)):
                rhs[pl.ds(part * 512 + q * 4 + g, 32, stride=16), :] = w
    total = FACTOR * jnp.dot(wide(rhs, 4), wide(lhs, 2), preferred_element_type=jnp.float32)
    for half in range(2):
        out[half * 512 : (half + 1) * 512, :] = total[:, half * 128 : (half + 1) * 128]
    for q in range(4):
        for half in range(2):
            v = [out[pl.ds(half * 512 + q * 4 + g, 32, stride=16), :] for g in range(4)]
            for r, w in enumerate(swap(v)):
                got_f[pl.ds((half * 4 + r) * 128 + q, 32, stride=4), :] = w
    back[...] = got_f[:1024, :].reshape(256, 4, 128).astype(jnp.bfloat16)


def multiply(got, right):
    return call(
        multiply_kernel,
        jax.ShapeDtypeStruct((256, 4, 128), jnp.bfloat16),
        [(2048, 128), (2048, 128), (1024, 128), (2048, 128), (1024, 128)],
        got, right,
    )


def unpack_kernel(mine, outgoing, incoming, held, rows):
    held[...] = mine[...].astype(jnp.float32).reshape(1024, 128)
    for product, ref in ((0, outgoing), (1, incoming)):
        for q in range(4):
            turned = flip(held[pl.ds(product * 512 + q, 128, stride=4), :].astype(jnp.bfloat16))
            for g in range(4):
                rows[pl.ds(q * 4 + g, 32, stride=16), :] = turned[g * 32 : (g + 1) * 32, :]
        ref[...] = rows[...].astype(jnp.bfloat16).reshape(32, 16, 128)


def unpack(mine):
    return call(
        unpack_kernel,
        (jax.ShapeDtypeStruct((32, 16, 128), jnp.bfloat16),) * 2,
        [(1024, 128), (512, 128)],
        mine,
    )


def body(out_left, out_right, in_left, in_right):
    got = lax.all_to_all(pack(out_left, out_right, in_left, in_right), CHIPS, 0, 0, tiled=True)
    right = lax.all_gather(got[:, 4:, :], "core", axis=0, tiled=False)
    back = multiply(got, right)
    return unpack(lax.all_to_all(back, CHIPS, 0, 0, tiled=True))


def solution(mesh):
    fine = Mesh(mesh.devices.reshape(2, 4, 2, 4, 8), ROW + COL)
    in_specs = (P(ROW, COL, None), P(COL, ROW, None), P(COL, ROW, None), P(ROW, COL, None))
    out_specs = (P(ROW, COL, None), P(ROW, COL, None))
    return jax.shard_map(body, mesh=fine, in_specs=in_specs, out_specs=out_specs, check_vma=False)
```

time: 88.7 us -> 78.6 us (0.89)
  local copies, waits for them, and re-layouts: 16.7 us -> 3.75 us
  Pallas kernels: 0 us -> 4.65 us
  other arithmetic: 1.07 us -> 0 us
    slice x6 -> x1, local copies, waits for them, and re-layouts: 7.57 us -> 0.14 us  [body(): right = lax.all_gather(got[:, 4:, :], 'core', axis=0, tiled=False)]
    pallas_call x0 -> x3, Pallas kernels: none -> 4.65 us  [call(): pl.pallas_call(kernel, out_shape=shape, in_specs=[pl.BlockSpec(memory_spa...]
    reshape x7 -> x0, local copies, waits for them, and re-layouts: 2.98 us -> none  [the longest x3 1.32 us: body(): result.reshape(8, 32, 32, 16).transpose(0, 2, 1, 3).reshape(256, 4, 128)]
    transpose x2 -> x0, local copies, waits for them, and re-layouts: 2.76 us -> none  [the longest x1 2.21 us: body(): result.reshape(8, 32, 32, 16).transpose(0, 2, 1, 3).reshape(256, 4, 128)]
    unnamed x2 -> x8, local copies, waits for them, and re-layouts: 1.92 us -> 3.61 us
    another operation x1 -> x0, other arithmetic: 1.02 us -> none  [body(): both = jnp.stack([left, right])]
where the time goes in v2:
time: 78.6 us; the launch traced here: 78.3 us
  blocking collectives  69.3 us (88%)
  Pallas kernels  4.65 us (6%)
  local copies, waits for them, and re-layouts  3.75 us (5%)
    all_to_all x1, blocking collectives, body(): lax.all_to_all(pack(out_left, out_right, in_left, in_right), CHIPS, 0, 0,...  42.8 us
    all_to_all x1, blocking collectives, body(): return unpack(lax.all_to_all(back, CHIPS, 0, 0, tiled=True))  24.3 us
    pallas_call x3, Pallas kernels, call(): pl.pallas_call(kernel, out_shape=shape, in_specs=[pl.BlockSpec(memory_spa...  4.65 us
    unnamed x8, local copies, waits for them, and re-layouts  3.61 us
    all_gather x1, blocking collectives, body(): right = lax.all_gather(got[:, 4:, :], 'core', axis=0, tiled=False)  2.18 us

profile of v2, /device:TPU:8, one launch (start us, length us, event | category | flops | bytes accessed | tf_op | source)
XLA Modules:
  0.0 78.3 jit_solution(1352246939057422249)
XLA Ops:
  0.6 0.0 copy-start
  0.6 0.9 %copy-done = bf16[32,16,128]{2,1,0:T(8,128)(2,1)S(1)} copy-done((bf16[32,16,128]{2,1,0:T(8,128)(2,1)S(1)}, bf16[32,16,128]{2,1,0:T(8,128)(2,1)}, u32[]{:S(2)}) %copy-start) | copy-done | bytes 131096
  1.5 0.0 copy-start.1
  1.5 0.9 %copy-done.1 = bf16[16,32,128]{2,1,0:T(8,128)(2,1)S(1)} copy-done((bf16[16,32,128]{2,1,0:T(8,128)(2,1)S(1)}, bf16[16,32,128]{2,1,0:T(8,128)(2,1)}, u32[]{:S(2)}) %copy-start.1) | copy-done | bytes 131096
  2.4 0.0 copy-start.2
  2.4 0.9 %copy-done.2 = bf16[16,32,128]{2,1,0:T(8,128)(2,1)S(1)} copy-done((bf16[16,32,128]{2,1,0:T(8,128)(2,1)S(1)}, bf16[16,32,128]{2,1,0:T(8,128)(2,1)}, u32[]{:S(2)}) %copy-start.2) | copy-done | bytes 131096
  3.3 0.0 copy-start.3
  3.3 0.9 %copy-done.3 = bf16[32,16,128]{2,1,0:T(8,128)(2,1)S(1)} copy-done((bf16[32,16,128]{2,1,0:T(8,128)(2,1)S(1)}, bf16[32,16,128]{2,1,0:T(8,128)(2,1)}, u32[]{:S(2)}) %copy-start.3) | copy-done | bytes 131096
  4.2 0.5 shard_map.59
  4.7 42.8 %all_to_all.10.got = bf16[256,8,128]{2,1,0:T(8,128)(2,1)S(1)} all-to-all(bf16[256,8,128]{2,1,0:T(8,128)(2,1)S(1)} %shard_map.59), channel_id=1, replica_groups=mesh['y_lo'=2,'x'=4,'core'=2,'y_hi'=4,'z'=8] {'y_lo','x','y_hi','z'}, dimensions={0} | all-to-all | bytes 1048576 | tf_op jit(solution)/shard_map/all_to_all | solution.py:141
  47.5 0.1 slice.4
  47.6 2.2 %all-gather = bf16[512,4,128]{2,1,0:T(4,128)(2,1)S(1)} all-gather(bf16[256,4,128]{2,1,0:T(4,128)(2,1)S(1)} %slice.4), channel_id=2, replica_groups=mesh['y_lo'=2,'x'=4,'core'=2,'y_hi'=4,'z'=8] {'core'}, dimensions={0}, use_global_device_ids=true | all-gather | bytes 786432 | tf_op jit(solution)/shard_map/all_gather | solution.py:142
  49.8 3.1 %shard_map.60 = bf16[256,4,128]{2,1,0:T(4,128)(2,1)S(1)} custom-call(bf16[256,8,128]{2,1,0:T(8,128)(2,1)S(1)} %all_to_all.10.got, bf16[2,256,4,128]{3,2,1,0:T(4,128)(2,1)S(1)} %bitcast.1), custom_call_target="tpu_custom_call" | custom-call | tf_op jit(solution)/shard_map/pallas_call | solution.py:18
  53.0 24.3 %all_to_all.11.mine = bf16[256,4,128]{2,1,0:T(4,128)(2,1)S(1)} all-to-all(bf16[256,4,128]{2,1,0:T(4,128)(2,1)S(1)} %shard_map.60), channel_id=1, replica_groups=mesh['y_lo'=2,'x'=4,'core'=2,'y_hi'=4,'z'=8] {'y_lo','x','y_hi','z'}, dimensions={0} | all-to-all | bytes 524288 | tf_op jit(solution)/shard_map/all_to_all | solution.py:144
  77.3 1.1 %shard_map.61 = (bf16[32,16,128]{2,1,0:T(8,128)(2,1)}, bf16[32,16,128]{2,1,0:T(8,128)(2,1)}) custom-call(bf16[256,4,128]{2,1,0:T(4,128)(2,1)S(1)} %all_to_all.11.mine), custom_call_target="tpu_custom_call" | custom-call | tf_op jit(solution)/shard_map/pallas_call | solution.py:18
Async XLA Ops:
  0.6 0.9 %copy-start = (bf16[32,16,128]{2,1,0:T(8,128)(2,1)S(1)}, bf16[32,16,128]{2,1,0:T(8,128)(2,1)}, u32[]{:S(2)}) copy-start(bf16[32,16,128]{2,1,0:T(8,128)(2,1)} %out_left.1) | copy-start | bytes 393220
  1.5 0.9 %copy-start.1 = (bf16[16,32,128]{2,1,0:T(8,128)(2,1)S(1)}, bf16[16,32,128]{2,1,0:T(8,128)(2,1)}, u32[]{:S(2)}) copy-start(bf16[16,32,128]{2,1,0:T(8,128)(2,1)} %out_right.1) | copy-start | bytes 393220
  2.4 0.9 %copy-start.2 = (bf16[16,32,128]{2,1,0:T(8,128)(2,1)S(1)}, bf16[16,32,128]{2,1,0:T(8,128)(2,1)}, u32[]{:S(2)}) copy-start(bf16[16,32,128]{2,1,0:T(8,128)(2,1)} %in_left.1) | copy-start | bytes 393220
  3.3 0.9 %copy-start.3 = (bf16[32,16,128]{2,1,0:T(8,128)(2,1)S(1)}, bf16[32,16,128]{2,1,0:T(8,128)(2,1)}, u32[]{:S(2)}) copy-start(bf16[32,16,128]{2,1,0:T(8,128)(2,1)} %in_right.1) | copy-start | bytes 393220

commit v3 on v2

v3 whole, which is shorter than its diff:
```python
import math

import jax
import jax.numpy as jnp
from jax import lax
from jax.experimental import pallas as pl
from jax.experimental.pallas import tpu as pltpu
from jax.sharding import Mesh, PartitionSpec as P

ROW = ("y_lo", "x", "core")
COL = ("y_hi", "z")
CHIPS = ("y_lo", "x", "y_hi", "z")
FACTOR = 1.0 / math.sqrt(512)
MIB = 1024 * 1024


def call(kernel, shape, scratch, *args, space=pltpu.VMEM, out_space=pltpu.VMEM, limit=32):
    return pl.pallas_call(
        kernel,
        out_shape=shape,
        in_specs=[pl.BlockSpec(memory_space=space)] * len(args),
        out_specs=jax.tree.map(lambda _: pl.BlockSpec(memory_space=out_space), shape),
        scratch_shapes=scratch,
        compiler_params=pltpu.CompilerParams(vmem_limit_bytes=limit * MIB),
    )(*args)


def f32(rows):
    return pltpu.VMEM((rows, 128), jnp.float32)


def flip(block):
    n = block.shape[1]
    eye = lax.broadcasted_iota(jnp.int32, (n, n), 0) == lax.broadcasted_iota(jnp.int32, (n, n), 1)
    eye = eye.astype(jnp.float32).astype(jnp.bfloat16)
    return lax.dot_general(eye, block, (((1,), (1,)), ((), ())), preferred_element_type=jnp.float32)


def swap(v):
    lane = lax.broadcasted_iota(jnp.int32, v[0].shape, 1)
    even, low = (lane // 32) % 2 == 0, lane < 64

    def pair(x, y, first, by):
        return (
            jnp.where(first, x, pltpu.roll(y, by, 1)),
            jnp.where(first, pltpu.roll(x, 128 - by, 1), y),
        )

    a0, a1 = pair(v[0], v[1], even, 32)
    a2, a3 = pair(v[2], v[3], even, 32)
    w0, w2 = pair(a0, a2, low, 64)
    w1, w3 = pair(a1, a3, low, 64)
    return w0, w1, w2, w3


def pack_kernel(blocks, sent, rows, held):
    for n, product, side, a_first in ((0, 0, 0, True), (1, 0, 1, False), (2, 1, 0, False), (3, 1, 1, True)):
        block = blocks[n]
        if a_first:
            rows[...] = block.astype(jnp.float32)
            block = jnp.concatenate([rows[pl.ds(b, 32, stride=16), :] for b in range(16)])
            block = block.astype(jnp.bfloat16)
        turned = flip(block)
        for q in range(4):
            held[pl.ds(product * 1024 + side * 4 + q, 128, stride=8), :] = turned[:, q * 128 : (q + 1) * 128]
    sent[...] = held[...].astype(jnp.bfloat16).reshape(256, 8, 128)


def pack(*blocks):
    return call(
        pack_kernel,
        jax.ShapeDtypeStruct((256, 8, 128), jnp.bfloat16),
        [f32(512), f32(2048)],
        jnp.stack([block.reshape(512, 128) for block in blocks]),
    )


def sort_kernel(got, left, right, got_f, sides):
    got_f[...] = got[...].astype(jnp.float32).reshape(2048, 128)
    for side, ref in ((1, right), (0, left)):
        for half in range(2):
            for q in range(4):
                v = [got_f[pl.ds((half * 4 + r) * 256 + side * 4 + q, 32, stride=8), :] for r in range(4)]
                for g, w in enumerate(swap(v)):
                    sides[pl.ds((side * 2 + half) * 512 + q * 4 + g, 32, stride=16), :] = w
            first = (side * 2 + half) * 512
            ref[:, half * 128 : (half + 1) * 128] = sides[first : first + 512, :].astype(jnp.bfloat16)


def sort(got):
    return call(
        sort_kernel,
        (jax.ShapeDtypeStruct((512, 256), jnp.bfloat16),) * 2,
        [f32(2048), f32(2048)],
        got,
    )


def multiply_kernel(left, right, back, out, held):
    total = None
    for core in range(2):
        lhs = jnp.concatenate([left[(2 * r + core) * 32 : (2 * r + core + 1) * 32, :] for r in range(8)])
        term = jnp.dot(right[core], lhs, preferred_element_type=jnp.float32)
        total = term if total is None else total + term
    total = total * FACTOR
    for half in range(2):
        out[half * 512 : (half + 1) * 512, :] = total[:, half * 128 : (half + 1) * 128]
        for q in range(4):
            v = [out[pl.ds(half * 512 + q * 4 + g, 32, stride=16), :] for g in range(4)]
            for r, w in enumerate(swap(v)):
                held[pl.ds((half * 4 + r) * 128 + q, 32, stride=4), :] = w
    back[...] = held[...].reshape(256, 4, 128).astype(jnp.bfloat16)


def multiply(left, right):
    return call(
        multiply_kernel,
        jax.ShapeDtypeStruct((256, 4, 128), jnp.bfloat16),
        [f32(1024), f32(1024)],
        left, right,
    )


def unpack_kernel(mine, outgoing, incoming, held, rows, done, sems):
    held[...] = mine[...].astype(jnp.float32).reshape(1024, 128)
    copies = []
    for product, ref in ((0, outgoing), (1, incoming)):
        for q in range(4):
            turned = flip(held[pl.ds(product * 512 + q, 128, stride=4), :].astype(jnp.bfloat16))
            for g in range(4):
                rows[pl.ds(product * 512 + q * 4 + g, 32, stride=16), :] = turned[g * 32 : (g + 1) * 32, :]
        block = rows[product * 512 : (product + 1) * 512, :].astype(jnp.bfloat16)
        done[product] = block.reshape(32, 16, 128)
        copies.append(pltpu.make_async_copy(done.at[product], ref, sems.at[product]))
        copies[-1].start()
    for copy in copies:
        copy.wait()


def unpack(mine):
    return call(
        unpack_kernel,
        (jax.ShapeDtypeStruct((32, 16, 128), jnp.bfloat16),) * 2,
        [f32(1024), f32(1024), pltpu.VMEM((2, 32, 16, 128), jnp.bfloat16), pltpu.SemaphoreType.DMA((2,))],
        mine, out_space=pltpu.HBM,
    )


def body(out_left, out_right, in_left, in_right):
    got = lax.all_to_all(pack(out_left, out_right, in_left, in_right), CHIPS, 0, 0, tiled=True)
    left, right = sort(got)
    both = lax.all_gather(right, "core", axis=0, tiled=False)
    back = multiply(left, both)
    return unpack(lax.all_to_all(back, CHIPS, 0, 0, tiled=True))


def solution(mesh):
    fine = Mesh(mesh.devices.reshape(2, 4, 2, 4, 8), ROW + COL)
    in_specs = (P(ROW, COL, None), P(COL, ROW, None), P(COL, ROW, None), P(ROW, COL, None))
    out_specs = (P(ROW, COL, None), P(ROW, COL, None))
    return jax.shard_map(body, mesh=fine, in_specs=in_specs, out_specs=out_specs, check_vma=False)
```

time: 78.6 us -> 75.1 us (0.955)
  local copies, waits for them, and re-layouts: 3.75 us -> 0 us
  other arithmetic: 0 us -> 1.16 us
  Pallas kernels: 4.65 us -> 3.73 us
    unnamed x8 -> x0, local copies, waits for them, and re-layouts: 3.61 us -> none
    another operation x0 -> x1, other arithmetic: none -> 1.16 us  [pack(): jnp.stack([block.reshape(512, 128) for block in blocks])]
    pallas_call x3 -> x4, Pallas kernels: 4.65 us -> 3.73 us  [call(): pl.pallas_call(kernel, out_shape=shape, in_specs=[pl.BlockSpec(memory_spa...]
where the time goes in v3:
time: 75.1 us; the launch traced here: 74.8 us
  blocking collectives  69.3 us (92%)
  Pallas kernels  3.73 us (5%)
  other arithmetic  1.16 us (2%)
    all_to_all x1, blocking collectives, body(): lax.all_to_all(pack(out_left, out_right, in_left, in_right), CHIPS, 0, 0,...  42.8 us
    all_to_all x1, blocking collectives, body(): return unpack(lax.all_to_all(back, CHIPS, 0, 0, tiled=True))  24.3 us
    pallas_call x4, Pallas kernels, call(): pl.pallas_call(kernel, out_shape=shape, in_specs=[pl.BlockSpec(memory_spa...  3.73 us
    all_gather x1, blocking collectives, body(): both = lax.all_gather(right, 'core', axis=0, tiled=False)  2.18 us

profile of v3, /device:TPU:8, one launch (start us, length us, event | category | flops | bytes accessed | tf_op | source)
XLA Modules:
  0.0 74.8 jit_solution(1431907505135340536)
XLA Ops:
  0.6 1.2 %pad_maximum_fusion.blocks = bf16[4,512,128]{2,1,0:T(8,128)(2,1)S(1)} fusion(bf16[1,512,128]{2,1,0:T(8,128)(2,1)} %bitcast.6, bf16[1,512,128]{2,1,0:T(8,128)(2,1)} %bitcast.7, bf16[1,512,128]{2,1,0:T(8,128)(2,1)} %bitcast.8, bf16[1,512,128]{2,1,0:T(8,128)(2,1)} %bitcast.9), kind=kLoop, calls=%fused_computation | loop fusion | flops 786432 | bytes 1048576 | tf_op jit(solution)/shard_map/stack | solution.py:74
  1.8 0.5 shard_map.59
  2.3 42.8 %all_to_all.10.got = bf16[256,8,128]{2,1,0:T(8,128)(2,1)S(1)} all-to-all(bf16[256,8,128]{2,1,0:T(8,128)(2,1)S(1)} %shard_map.59), channel_id=1, replica_groups=mesh['y_lo'=2,'x'=4,'core'=2,'y_hi'=4,'z'=8] {'y_lo','x','y_hi','z'}, dimensions={0} | all-to-all | bytes 1048576 | tf_op jit(solution)/shard_map/all_to_all | solution.py:150
  45.0 1.6 %shard_map.60 = (bf16[512,256]{1,0:T(8,128)(2,1)S(1)}, bf16[512,256]{1,0:T(8,128)(2,1)S(1)}) custom-call(bf16[256,8,128]{2,1,0:T(8,128)(2,1)S(1)} %all_to_all.10.got), custom_call_target="tpu_custom_call" | custom-call | tf_op jit(solution)/shard_map/pallas_call | solution.py:18
  46.6 2.2 %all-gather = bf16[1024,256]{1,0:T(8,128)(2,1)S(1)} all-gather(bf16[512,256]{1,0:T(8,128)(2,1)S(1)} %get-tuple-element.5), channel_id=2, replica_groups=mesh['y_lo'=2,'x'=4,'core'=2,'y_hi'=4,'z'=8] {'core'}, dimensions={0}, use_global_device_ids=true | all-gather | bytes 786432 | tf_op jit(solution)/shard_map/all_gather | solution.py:152
  48.8 0.6 shard_map.61
  49.5 24.3 %all_to_all.11.mine = bf16[256,4,128]{2,1,0:T(4,128)(2,1)S(1)} all-to-all(bf16[256,4,128]{2,1,0:T(4,128)(2,1)S(1)} %shard_map.61), channel_id=1, replica_groups=mesh['y_lo'=2,'x'=4,'core'=2,'y_hi'=4,'z'=8] {'y_lo','x','y_hi','z'}, dimensions={0} | all-to-all | bytes 524288 | tf_op jit(solution)/shard_map/all_to_all | solution.py:154
  73.8 1.1 %shard_map.62 = (bf16[32,16,128]{2,1,0:T(8,128)(2,1)}, bf16[32,16,128]{2,1,0:T(8,128)(2,1)}) custom-call(bf16[256,4,128]{2,1,0:T(4,128)(2,1)S(1)} %all_to_all.11.mine), custom_call_target="tpu_custom_call" | custom-call | tf_op jit(solution)/shard_map/pallas_call | solution.py:18

commit v4 on v3

--- a/solution.py
+++ b/solution.py
@@ -10,6 +10,7 @@
 ROW = ("y_lo", "x", "core")
 COL = ("y_hi", "z")
 CHIPS = ("y_lo", "x", "y_hi", "z")
+STEP = {"y_lo": 128, "x": 32, "z": 1}
 FACTOR = 1.0 / math.sqrt(512)
 MIB = 1024 * 1024
 
@@ -75,28 +76,37 @@
     )
 
 
-def sort_kernel(got, left, right, got_f, sides):
+def chip_row(half, r):
+    return half * STEP["y_lo"] + r * STEP["x"]
+
+
+def sort_kernel(got, left, right, got_f, sorted_f):
     got_f[...] = got[...].astype(jnp.float32).reshape(2048, 128)
-    for side, ref in ((1, right), (0, left)):
+    for side in (1, 0):
         for half in range(2):
+            lanes = slice(half * 128, (half + 1) * 128)
             for q in range(4):
-                v = [got_f[pl.ds((half * 4 + r) * 256 + side * 4 + q, 32, stride=8), :] for r in range(4)]
+                v = [got_f[pl.ds(chip_row(half, r) * 8 + side * 4 + q, 32, stride=STEP["z"] * 8), :] for r in range(4)]
                 for g, w in enumerate(swap(v)):
-                    sides[pl.ds((side * 2 + half) * 512 + q * 4 + g, 32, stride=16), :] = w
-            first = (side * 2 + half) * 512
-            ref[:, half * 128 : (half + 1) * 128] = sides[first : first + 512, :].astype(jnp.bfloat16)
+                    b = q * 4 + g
+                    if side == 1:
+                        right[b * 32 : (b + 1) * 32, lanes] = w.astype(jnp.bfloat16)
+                    else:
+                        sorted_f[pl.ds(half * 512 + b, 32, stride=16), :] = w
+            if side == 0:
+                left[:, lanes] = sorted_f[half * 512 : (half + 1) * 512, :].astype(jnp.bfloat16)
 
 
 def sort(got):
     return call(
         sort_kernel,
         (jax.ShapeDtypeStruct((512, 256), jnp.bfloat16),) * 2,
-        [f32(2048), f32(2048)],
+        [f32(2048), f32(1024)],
         got,
     )
 
 
-def multiply_kernel(left, right, back, out, held):
+def multiply_kernel(left, right, back, held):
     total = None
     for core in range(2):
         lhs = jnp.concatenate([left[(2 * r + core) * 32 : (2 * r + core + 1) * 32, :] for r in range(8)])
@@ -104,11 +114,10 @@
         total = term if total is None else total + term
     total = total * FACTOR
     for half in range(2):
-        out[half * 512 : (half + 1) * 512, :] = total[:, half * 128 : (half + 1) * 128]
         for q in range(4):
-            v = [out[pl.ds(half * 512 + q * 4 + g, 32, stride=16), :] for g in range(4)]
+            v = [total[(q * 4 + g) * 32 : (q * 4 + g + 1) * 32, half * 128 : (half + 1) * 128] for g in range(4)]
             for r, w in enumerate(swap(v)):
-                held[pl.ds((half * 4 + r) * 128 + q, 32, stride=4), :] = w
+                held[pl.ds(chip_row(half, r) * 4 + q, 32, stride=STEP["z"] * 4), :] = w
     back[...] = held[...].reshape(256, 4, 128).astype(jnp.bfloat16)
 
 
@@ -116,7 +125,7 @@
     return call(
         multiply_kernel,
         jax.ShapeDtypeStruct((256, 4, 128), jnp.bfloat16),
-        [f32(1024), f32(1024)],
+        [f32(1024)],
         left, right,
     )
 

time: 75.1 us -> 74.7 us (level)
  no operation moved by 1% of the time
where the time goes in v4:
time: 74.7 us; the launch traced here: 74.4 us
  blocking collectives  69.3 us (93%)
  Pallas kernels  3.32 us (4%)
  other arithmetic  1.16 us (2%)
    all_to_all x1, blocking collectives, body(): lax.all_to_all(pack(out_left, out_right, in_left, in_right), CHIPS, 0, 0,...  42.8 us
    all_to_all x1, blocking collectives, body(): return unpack(lax.all_to_all(back, CHIPS, 0, 0, tiled=True))  24.3 us
    pallas_call x4, Pallas kernels, call(): pl.pallas_call(kernel, out_shape=shape, in_specs=[pl.BlockSpec(memory_spa...  3.32 us
    all_gather x1, blocking collectives, body(): both = lax.all_gather(right, 'core', axis=0, tiled=False)  2.18 us

profile of v4, /device:TPU:8, one launch (start us, length us, event | category | flops | bytes accessed | tf_op | source)
XLA Modules:
  0.0 74.4 jit_solution(11590901369732218663)
XLA Ops:
  0.6 1.2 %pad_maximum_fusion.blocks = bf16[4,512,128]{2,1,0:T(8,128)(2,1)S(1)} fusion(bf16[1,512,128]{2,1,0:T(8,128)(2,1)} %bitcast.6, bf16[1,512,128]{2,1,0:T(8,128)(2,1)} %bitcast.7, bf16[1,512,128]{2,1,0:T(8,128)(2,1)} %bitcast.8, bf16[1,512,128]{2,1,0:T(8,128)(2,1)} %bitcast.9), kind=kLoop, calls=%fused_computation | loop fusion | flops 786432 | bytes 1048576 | tf_op jit(solution)/shard_map/stack | solution.py:75
  1.8 0.5 shard_map.59
  2.3 42.8 %all_to_all.10.got = bf16[256,8,128]{2,1,0:T(8,128)(2,1)S(1)} all-to-all(bf16[256,8,128]{2,1,0:T(8,128)(2,1)S(1)} %shard_map.59), channel_id=1, replica_groups=mesh['y_lo'=2,'x'=4,'core'=2,'y_hi'=4,'z'=8] {'y_lo','x','y_hi','z'}, dimensions={0} | all-to-all | bytes 1048576 | tf_op jit(solution)/shard_map/all_to_all | solution.py:159
  45.0 1.2 %shard_map.60 = (bf16[512,256]{1,0:T(8,128)(2,1)S(1)}, bf16[512,256]{1,0:T(8,128)(2,1)S(1)}) custom-call(bf16[256,8,128]{2,1,0:T(8,128)(2,1)S(1)} %all_to_all.10.got), custom_call_target="tpu_custom_call" | custom-call | tf_op jit(solution)/shard_map/pallas_call | solution.py:19
  46.3 2.2 %all-gather = bf16[1024,256]{1,0:T(8,128)(2,1)S(1)} all-gather(bf16[512,256]{1,0:T(8,128)(2,1)S(1)} %get-tuple-element.5), channel_id=2, replica_groups=mesh['y_lo'=2,'x'=4,'core'=2,'y_hi'=4,'z'=8] {'core'}, dimensions={0}, use_global_device_ids=true | all-gather | bytes 786432 | tf_op jit(solution)/shard_map/all_gather | solution.py:161
  48.5 0.6 shard_map.61
  49.0 24.3 %all_to_all.11.mine = bf16[256,4,128]{2,1,0:T(4,128)(2,1)S(1)} all-to-all(bf16[256,4,128]{2,1,0:T(4,128)(2,1)S(1)} %shard_map.61), channel_id=1, replica_groups=mesh['y_lo'=2,'x'=4,'core'=2,'y_hi'=4,'z'=8] {'y_lo','x','y_hi','z'}, dimensions={0} | all-to-all | bytes 524288 | tf_op jit(solution)/shard_map/all_to_all | solution.py:163
  73.4 1.1 %shard_map.62 = (bf16[32,16,128]{2,1,0:T(8,128)(2,1)}, bf16[32,16,128]{2,1,0:T(8,128)(2,1)}) custom-call(bf16[256,4,128]{2,1,0:T(4,128)(2,1)S(1)} %all_to_all.11.mine), custom_call_target="tpu_custom_call" | custom-call | tf_op jit(solution)/shard_map/pallas_call | solution.py:19

commit v5 on v4

--- a/solution.py
+++ b/solution.py
@@ -40,17 +40,18 @@
 def swap(v):
     lane = lax.broadcasted_iota(jnp.int32, v[0].shape, 1)
     even, low = (lane // 32) % 2 == 0, lane < 64
+    middle = (lane >= 32) & (lane < 96)
 
-    def pair(x, y, first, by):
-        return (
-            jnp.where(first, x, pltpu.roll(y, by, 1)),
-            jnp.where(first, pltpu.roll(x, 128 - by, 1), y),
-        )
+    def pair(x, y):
+        moved = pltpu.roll(jnp.where(even, y, x), 32, 1)
+        return jnp.where(even, x, moved), jnp.where(even, moved, y)
 
-    a0, a1 = pair(v[0], v[1], even, 32)
-    a2, a3 = pair(v[2], v[3], even, 32)
-    w0, w2 = pair(a0, a2, low, 64)
-    w1, w3 = pair(a1, a3, low, 64)
+    a0, a1 = pair(v[0], v[1])
+    a2, a3 = pair(v[2], v[3])
+    moved = pltpu.roll(jnp.where(low, a2, a0), 64, 1)
+    w0, w2 = jnp.where(low, a0, moved), jnp.where(low, moved, a2)
+    moved, kept = pltpu.roll(jnp.where(low, a3, a1), 64, 1), jnp.where(low, a1, a3)
+    w1, w3 = jnp.where(middle, kept, moved), jnp.where(middle, moved, kept)
     return w0, w1, w2, w3
 
 

time: 74.7 us -> 74.1 us (level)
  no operation moved by 1% of the time
where the time goes in v5:
time: 74.1 us; the launch traced here: 73.9 us
  blocking collectives  69.3 us (94%)
  Pallas kernels  2.76 us (4%)
  other arithmetic  1.16 us (2%)
    all_to_all x1, blocking collectives, body(): lax.all_to_all(pack(out_left, out_right, in_left, in_right), CHIPS, 0, 0,...  42.8 us
    all_to_all x1, blocking collectives, body(): return unpack(lax.all_to_all(back, CHIPS, 0, 0, tiled=True))  24.3 us
    pallas_call x4, Pallas kernels, call(): pl.pallas_call(kernel, out_shape=shape, in_specs=[pl.BlockSpec(memory_spa...  2.76 us
    all_gather x1, blocking collectives, body(): both = lax.all_gather(right, 'core', axis=0, tiled=False)  2.18 us

profile of v5, /device:TPU:8, one launch (start us, length us, event | category | flops | bytes accessed | tf_op | source)
XLA Modules:
  0.0 73.9 jit_solution(3123374659338463049)
XLA Ops:
  0.6 1.2 %pad_maximum_fusion.blocks = bf16[4,512,128]{2,1,0:T(8,128)(2,1)S(1)} fusion(bf16[1,512,128]{2,1,0:T(8,128)(2,1)} %bitcast.6, bf16[1,512,128]{2,1,0:T(8,128)(2,1)} %bitcast.7, bf16[1,512,128]{2,1,0:T(8,128)(2,1)} %bitcast.8, bf16[1,512,128]{2,1,0:T(8,128)(2,1)} %bitcast.9), kind=kLoop, calls=%fused_computation | loop fusion | flops 786432 | bytes 1048576 | tf_op jit(solution)/shard_map/stack | solution.py:76
  1.8 0.5 shard_map.59
  2.3 42.8 %all_to_all.10.got = bf16[256,8,128]{2,1,0:T(8,128)(2,1)S(1)} all-to-all(bf16[256,8,128]{2,1,0:T(8,128)(2,1)S(1)} %shard_map.59), channel_id=1, replica_groups=mesh['y_lo'=2,'x'=4,'core'=2,'y_hi'=4,'z'=8] {'y_lo','x','y_hi','z'}, dimensions={0} | all-to-all | bytes 1048576 | tf_op jit(solution)/shard_map/all_to_all | solution.py:160
  45.0 0.7 shard_map.60
  45.8 2.2 %all-gather = bf16[1024,256]{1,0:T(8,128)(2,1)S(1)} all-gather(bf16[512,256]{1,0:T(8,128)(2,1)S(1)} %get-tuple-element.5), channel_id=2, replica_groups=mesh['y_lo'=2,'x'=4,'core'=2,'y_hi'=4,'z'=8] {'core'}, dimensions={0}, use_global_device_ids=true | all-gather | bytes 786432 | tf_op jit(solution)/shard_map/all_gather | solution.py:162
  48.0 0.5 shard_map.61
  48.5 24.3 %all_to_all.11.mine = bf16[256,4,128]{2,1,0:T(4,128)(2,1)S(1)} all-to-all(bf16[256,4,128]{2,1,0:T(4,128)(2,1)S(1)} %shard_map.61), channel_id=1, replica_groups=mesh['y_lo'=2,'x'=4,'core'=2,'y_hi'=4,'z'=8] {'y_lo','x','y_hi','z'}, dimensions={0} | all-to-all | bytes 524288 | tf_op jit(solution)/shard_map/all_to_all | solution.py:164
  72.8 1.1 %shard_map.62 = (bf16[32,16,128]{2,1,0:T(8,128)(2,1)}, bf16[32,16,128]{2,1,0:T(8,128)(2,1)}) custom-call(bf16[256,4,128]{2,1,0:T(4,128)(2,1)S(1)} %all_to_all.11.mine), custom_call_target="tpu_custom_call" | custom-call | tf_op jit(solution)/shard_map/pallas_call | solution.py:19

commit v6 on v5

--- a/solution.py
+++ b/solution.py
@@ -9,8 +9,8 @@
 
 ROW = ("y_lo", "x", "core")
 COL = ("y_hi", "z")
-CHIPS = ("y_lo", "x", "y_hi", "z")
-STEP = {"y_lo": 128, "x": 32, "z": 1}
+CHIPS = ("y_hi", "y_lo", "z", "x")
+STEP = {"y_hi": 64, "y_lo": 32, "z": 4, "x": 1}
 FACTOR = 1.0 / math.sqrt(512)
 MIB = 1024 * 1024
 
@@ -77,8 +77,9 @@
     )
 
 
-def chip_row(half, r):
-    return half * STEP["y_lo"] + r * STEP["x"]
+def chip_rows(half, r, y, height, row):
+    first = half * STEP["y_lo"] + r * STEP["x"] + y * STEP["y_hi"]
+    return pl.ds(first * height + row, 8, stride=STEP["z"] * height)
 
 
 def sort_kernel(got, left, right, got_f, sorted_f):
@@ -87,7 +88,10 @@
         for half in range(2):
             lanes = slice(half * 128, (half + 1) * 128)
             for q in range(4):
-                v = [got_f[pl.ds(chip_row(half, r) * 8 + side * 4 + q, 32, stride=STEP["z"] * 8), :] for r in range(4)]
+                v = [
+                    jnp.concatenate([got_f[chip_rows(half, r, y, 8, side * 4 + q), :] for y in range(4)])
+                    for r in range(4)
+                ]
                 for g, w in enumerate(swap(v)):
                     b = q * 4 + g
                     if side == 1:
@@ -118,7 +122,8 @@
         for q in range(4):
             v = [total[(q * 4 + g) * 32 : (q * 4 + g + 1) * 32, half * 128 : (half + 1) * 128] for g in range(4)]
             for r, w in enumerate(swap(v)):
-                held[pl.ds(chip_row(half, r) * 4 + q, 32, stride=STEP["z"] * 4), :] = w
+                for y in range(4):
+                    held[chip_rows(half, r, y, 4, q), :] = w[y * 8 : (y + 1) * 8, :]
     back[...] = held[...].reshape(256, 4, 128).astype(jnp.bfloat16)
 
 

time: 74.1 us -> 73.5 us (level)
  blocking collectives: 69.3 us -> 68.4 us
    all_to_all x1, blocking collectives: 42.8 us -> 41.6 us  [body(): lax.all_to_all(pack(out_left, out_right, in_left, in_right), CHIPS, 0, 0,...]
where the time goes in v6:
time: 73.5 us; the launch traced here: 73.3 us
  blocking collectives  68.4 us (93%)
  Pallas kernels  3.07 us (4%)
  other arithmetic  1.16 us (2%)
    all_to_all x1, blocking collectives, body(): lax.all_to_all(pack(out_left, out_right, in_left, in_right), CHIPS, 0, 0,...  41.6 us
    all_to_all x1, blocking collectives, body(): return unpack(lax.all_to_all(back, CHIPS, 0, 0, tiled=True))  24.6 us
    pallas_call x4, Pallas kernels, call(): pl.pallas_call(kernel, out_shape=shape, in_specs=[pl.BlockSpec(memory_spa...  3.07 us
    all_gather x1, blocking collectives, body(): both = lax.all_gather(right, 'core', axis=0, tiled=False)  2.18 us

profile of v6, /device:TPU:8, one launch (start us, length us, event | category | flops | bytes accessed | tf_op | source)
XLA Modules:
  0.0 73.3 jit_solution(18258964263538289328)
XLA Ops:
  0.6 1.2 %pad_maximum_fusion.blocks = bf16[4,512,128]{2,1,0:T(8,128)(2,1)S(1)} fusion(bf16[1,512,128]{2,1,0:T(8,128)(2,1)} %bitcast.6, bf16[1,512,128]{2,1,0:T(8,128)(2,1)} %bitcast.7, bf16[1,512,128]{2,1,0:T(8,128)(2,1)} %bitcast.8, bf16[1,512,128]{2,1,0:T(8,128)(2,1)} %bitcast.9), kind=kLoop, calls=%fused_computation | loop fusion | flops 786432 | bytes 1048576 | tf_op jit(solution)/shard_map/stack | solution.py:76
  1.8 0.5 shard_map.59
  2.3 41.6 %all_to_all.10.got = bf16[256,8,128]{2,1,0:T(8,128)(2,1)S(1)} all-to-all(bf16[256,8,128]{2,1,0:T(8,128)(2,1)S(1)} %shard_map.59), channel_id=1, replica_groups=mesh['y_lo'=2,'x'=4,'core'=2,'y_hi'=4,'z'=8] {'y_hi','y_lo','z','x'}, dimensions={0} | all-to-all | bytes 1048576 | tf_op jit(solution)/shard_map/all_to_all | solution.py:165
  43.9 1.0 %shard_map.60 = (bf16[512,256]{1,0:T(8,128)(2,1)S(1)}, bf16[512,256]{1,0:T(8,128)(2,1)S(1)}) custom-call(bf16[256,8,128]{2,1,0:T(8,128)(2,1)S(1)} %all_to_all.10.got), custom_call_target="tpu_custom_call" | custom-call | tf_op jit(solution)/shard_map/pallas_call | solution.py:19
  44.9 2.2 %all-gather = bf16[1024,256]{1,0:T(8,128)(2,1)S(1)} all-gather(bf16[512,256]{1,0:T(8,128)(2,1)S(1)} %get-tuple-element.5), channel_id=2, replica_groups=mesh['y_lo'=2,'x'=4,'core'=2,'y_hi'=4,'z'=8] {'core'}, dimensions={0}, use_global_device_ids=true | all-gather | bytes 786432 | tf_op jit(solution)/shard_map/all_gather | solution.py:167
  47.1 0.6 shard_map.61
  47.6 24.6 %all_to_all.11.mine = bf16[256,4,128]{2,1,0:T(4,128)(2,1)S(1)} all-to-all(bf16[256,4,128]{2,1,0:T(4,128)(2,1)S(1)} %shard_map.61), channel_id=1, replica_groups=mesh['y_lo'=2,'x'=4,'core'=2,'y_hi'=4,'z'=8] {'y_hi','y_lo','z','x'}, dimensions={0} | all-to-all | bytes 524288 | tf_op jit(solution)/shard_map/all_to_all | solution.py:169
  72.2 1.1 %shard_map.62 = (bf16[32,16,128]{2,1,0:T(8,128)(2,1)}, bf16[32,16,128]{2,1,0:T(8,128)(2,1)}) custom-call(bf16[256,4,128]{2,1,0:T(4,128)(2,1)S(1)} %all_to_all.11.mine), custom_call_target="tpu_custom_call" | custom-call | tf_op jit(solution)/shard_map/pallas_call | solution.py:19

commit v7 on v6

--- a/solution.py
+++ b/solution.py
@@ -30,13 +30,6 @@
     return pltpu.VMEM((rows, 128), jnp.float32)
 
 
-def flip(block):
-    n = block.shape[1]
-    eye = lax.broadcasted_iota(jnp.int32, (n, n), 0) == lax.broadcasted_iota(jnp.int32, (n, n), 1)
-    eye = eye.astype(jnp.float32).astype(jnp.bfloat16)
-    return lax.dot_general(eye, block, (((1,), (1,)), ((), ())), preferred_element_type=jnp.float32)
-
-
 def swap(v):
     lane = lax.broadcasted_iota(jnp.int32, v[0].shape, 1)
     even, low = (lane // 32) % 2 == 0, lane < 64
@@ -62,7 +55,7 @@
             rows[...] = block.astype(jnp.float32)
             block = jnp.concatenate([rows[pl.ds(b, 32, stride=16), :] for b in range(16)])
             block = block.astype(jnp.bfloat16)
-        turned = flip(block)
+        turned = block.astype(jnp.float32).T
         for q in range(4):
             held[pl.ds(product * 1024 + side * 4 + q, 128, stride=8), :] = turned[:, q * 128 : (q + 1) * 128]
     sent[...] = held[...].astype(jnp.bfloat16).reshape(256, 8, 128)
@@ -77,19 +70,23 @@
     )
 
 
-def chip_rows(half, r, y, height, row):
+def chip_rows(half, r, y, q):
     first = half * STEP["y_lo"] + r * STEP["x"] + y * STEP["y_hi"]
-    return pl.ds(first * height + row, 8, stride=STEP["z"] * height)
+    return pl.ds(first * 4 + q, 8, stride=STEP["z"] * 4)
 
 
 def sort_kernel(got, left, right, got_f, sorted_f):
-    got_f[...] = got[...].astype(jnp.float32).reshape(2048, 128)
+    tiles = got[...].astype(jnp.float32).reshape(64, 4, 8, 128)
+    for r in range(4):
+        got_f[r * 512 : (r + 1) * 512, :] = tiles[:, r].reshape(512, 128)
     for side in (1, 0):
         for half in range(2):
             lanes = slice(half * 128, (half + 1) * 128)
             for q in range(4):
                 v = [
-                    jnp.concatenate([got_f[chip_rows(half, r, y, 8, side * 4 + q), :] for y in range(4)])
+                    jnp.concatenate(
+                        [got_f[pl.ds((r * 64 + y * 16 + half * 8) * 8 + side * 4 + q, 8, stride=8), :] for y in range(4)]
+                    )
                     for r in range(4)
                 ]
                 for g, w in enumerate(swap(v)):
@@ -123,7 +120,7 @@
             v = [total[(q * 4 + g) * 32 : (q * 4 + g + 1) * 32, half * 128 : (half + 1) * 128] for g in range(4)]
             for r, w in enumerate(swap(v)):
                 for y in range(4):
-                    held[chip_rows(half, r, y, 4, q), :] = w[y * 8 : (y + 1) * 8, :]
+                    held[chip_rows(half, r, y, q), :] = w[y * 8 : (y + 1) * 8, :]
     back[...] = held[...].reshape(256, 4, 128).astype(jnp.bfloat16)
 
 
@@ -141,7 +138,7 @@
     copies = []
     for product, ref in ((0, outgoing), (1, incoming)):
         for q in range(4):
-            turned = flip(held[pl.ds(product * 512 + q, 128, stride=4), :].astype(jnp.bfloat16))
+            turned = held[pl.ds(product * 512 + q, 128, stride=4), :].T
             for g in range(4):
                 rows[pl.ds(product * 512 + q * 4 + g, 32, stride=16), :] = turned[g * 32 : (g + 1) * 32, :]
         block = rows[product * 512 : (product + 1) * 512, :].astype(jnp.bfloat16)

time: 73.5 us -> 73 us (level)
  no operation moved by 1% of the time
where the time goes in v7:
time: 73 us; the launch traced here: 72.8 us
  blocking collectives  68.4 us (94%)
  Pallas kernels  2.6 us (4%)
  other arithmetic  1.16 us (2%)
    all_to_all x1, blocking collectives, body(): lax.all_to_all(pack(out_left, out_right, in_left, in_right), CHIPS, 0, 0,...  41.6 us
    all_to_all x1, blocking collectives, body(): return unpack(lax.all_to_all(back, CHIPS, 0, 0, tiled=True))  24.6 us
    pallas_call x4, Pallas kernels, call(): pl.pallas_call(kernel, out_shape=shape, in_specs=[pl.BlockSpec(memory_spa...  2.6 us
    all_gather x1, blocking collectives, body(): both = lax.all_gather(right, 'core', axis=0, tiled=False)  2.18 us

profile of v7, /device:TPU:8, one launch (start us, length us, event | category | flops | bytes accessed | tf_op | source)
XLA Modules:
  0.0 72.8 jit_solution(6792822519327754929)
XLA Ops:
  0.6 1.2 %pad_maximum_fusion.blocks = bf16[4,512,128]{2,1,0:T(8,128)(2,1)S(1)} fusion(bf16[1,512,128]{2,1,0:T(8,128)(2,1)} %bitcast.6, bf16[1,512,128]{2,1,0:T(8,128)(2,1)} %bitcast.7, bf16[1,512,128]{2,1,0:T(8,128)(2,1)} %bitcast.8, bf16[1,512,128]{2,1,0:T(8,128)(2,1)} %bitcast.9), kind=kLoop, calls=%fused_computation | loop fusion | flops 786432 | bytes 1048576 | tf_op jit(solution)/shard_map/stack | solution.py:69
  1.8 0.4 shard_map.59
  2.2 41.6 %all_to_all.10.got = bf16[256,8,128]{2,1,0:T(8,128)(2,1)S(1)} all-to-all(bf16[256,8,128]{2,1,0:T(8,128)(2,1)S(1)} %shard_map.59), channel_id=1, replica_groups=mesh['y_lo'=2,'x'=4,'core'=2,'y_hi'=4,'z'=8] {'y_hi','y_lo','z','x'}, dimensions={0} | all-to-all | bytes 1048576 | tf_op jit(solution)/shard_map/all_to_all | solution.py:162
  43.8 0.7 shard_map.60
  44.5 2.2 %all-gather = bf16[1024,256]{1,0:T(8,128)(2,1)S(1)} all-gather(bf16[512,256]{1,0:T(8,128)(2,1)S(1)} %get-tuple-element.5), channel_id=2, replica_groups=mesh['y_lo'=2,'x'=4,'core'=2,'y_hi'=4,'z'=8] {'core'}, dimensions={0}, use_global_device_ids=true | all-gather | bytes 786432 | tf_op jit(solution)/shard_map/all_gather | solution.py:164
  46.7 0.6 shard_map.61
  47.3 24.6 %all_to_all.11.mine = bf16[256,4,128]{2,1,0:T(4,128)(2,1)S(1)} all-to-all(bf16[256,4,128]{2,1,0:T(4,128)(2,1)S(1)} %shard_map.61), channel_id=1, replica_groups=mesh['y_lo'=2,'x'=4,'core'=2,'y_hi'=4,'z'=8] {'y_hi','y_lo','z','x'}, dimensions={0} | all-to-all | bytes 524288 | tf_op jit(solution)/shard_map/all_to_all | solution.py:166
  71.9 0.9 %shard_map.62 = (bf16[32,16,128]{2,1,0:T(8,128)(2,1)}, bf16[32,16,128]{2,1,0:T(8,128)(2,1)}) custom-call(bf16[256,4,128]{2,1,0:T(4,128)(2,1)S(1)} %all_to_all.11.mine), custom_call_target="tpu_custom_call" | custom-call | tf_op jit(solution)/shard_map/pallas_call | solution.py:19

commit v8 on v7

--- a/solution.py
+++ b/solution.py
@@ -66,7 +66,7 @@
         pack_kernel,
         jax.ShapeDtypeStruct((256, 8, 128), jnp.bfloat16),
         [f32(512), f32(2048)],
-        jnp.stack([block.reshape(512, 128) for block in blocks]),
+        jnp.concatenate([block.reshape(512, 128) for block in blocks]).reshape(4, 512, 128),
     )
 
 
@@ -134,9 +134,10 @@
 
 
 def unpack_kernel(mine, outgoing, incoming, held, rows, done, sems):
-    held[...] = mine[...].astype(jnp.float32).reshape(1024, 128)
     copies = []
     for product, ref in ((0, outgoing), (1, incoming)):
+        part = slice(product * 512, (product + 1) * 512)
+        held[part, :] = mine[product * 128 : (product + 1) * 128].astype(jnp.float32).reshape(512, 128)
         for q in range(4):
             turned = held[pl.ds(product * 512 + q, 128, stride=4), :].T
             for g in range(4):

time: 73 us -> 73 us (level)
    another operation x1 -> x0, other arithmetic: 1.16 us -> none  [pack(): jnp.stack([block.reshape(512, 128) for block in blocks])]
    concatenate x0 -> x1, other arithmetic: none -> 1.13 us  [pack(): jnp.concatenate([block.reshape(512, 128) for block in blocks])]
where the time goes in v8:
time: 73 us; the launch traced here: 72.8 us
  blocking collectives  68.4 us (94%)
  Pallas kernels  2.59 us (4%)
  other arithmetic  1.13 us (2%)
    all_to_all x1, blocking collectives, body(): lax.all_to_all(pack(out_left, out_right, in_left, in_right), CHIPS, 0, 0,...  41.6 us
    all_to_all x1, blocking collectives, body(): return unpack(lax.all_to_all(back, CHIPS, 0, 0, tiled=True))  24.6 us
    pallas_call x4, Pallas kernels, call(): pl.pallas_call(kernel, out_shape=shape, in_specs=[pl.BlockSpec(memory_spa...  2.59 us
    all_gather x1, blocking collectives, body(): both = lax.all_gather(right, 'core', axis=0, tiled=False)  2.18 us

profile of v8, /device:TPU:8, one launch (start us, length us, event | category | flops | bytes accessed | tf_op | source)
XLA Modules:
  0.0 72.8 jit_solution(6811090986938257951)
XLA Ops:
  0.6 1.1 %pad_maximum_fusion = bf16[2048,128]{1,0:T(8,128)(2,1)S(1)} fusion(bf16[512,128]{1,0:T(8,128)(2,1)} %bitcast.8, bf16[512,128]{1,0:T(8,128)(2,1)} %bitcast.9, bf16[512,128]{1,0:T(8,128)(2,1)} %bitcast.10, bf16[512,128]{1,0:T(8,128)(2,1)} %bitcast.11), kind=kLoop, calls=%fused_computation | loop fusion | flops 2097152 | bytes 1048576 | tf_op jit(solution)/shard_map/concatenate | solution.py:69
  1.8 0.4 shard_map.59
  2.1 41.6 %all_to_all.10.got = bf16[256,8,128]{2,1,0:T(8,128)(2,1)S(1)} all-to-all(bf16[256,8,128]{2,1,0:T(8,128)(2,1)S(1)} %shard_map.59), channel_id=1, replica_groups=mesh['y_lo'=2,'x'=4,'core'=2,'y_hi'=4,'z'=8] {'y_hi','y_lo','z','x'}, dimensions={0} | all-to-all | bytes 1048576 | tf_op jit(solution)/shard_map/all_to_all | solution.py:163
  43.8 0.7 shard_map.60
  44.5 2.2 %all-gather = bf16[1024,256]{1,0:T(8,128)(2,1)S(1)} all-gather(bf16[512,256]{1,0:T(8,128)(2,1)S(1)} %get-tuple-element.5), channel_id=2, replica_groups=mesh['y_lo'=2,'x'=4,'core'=2,'y_hi'=4,'z'=8] {'core'}, dimensions={0}, use_global_device_ids=true | all-gather | bytes 786432 | tf_op jit(solution)/shard_map/all_gather | solution.py:165
  46.7 0.6 shard_map.61
  47.3 24.6 %all_to_all.11.mine = bf16[256,4,128]{2,1,0:T(4,128)(2,1)S(1)} all-to-all(bf16[256,4,128]{2,1,0:T(4,128)(2,1)S(1)} %shard_map.61), channel_id=1, replica_groups=mesh['y_lo'=2,'x'=4,'core'=2,'y_hi'=4,'z'=8] {'y_hi','y_lo','z','x'}, dimensions={0} | all-to-all | bytes 524288 | tf_op jit(solution)/shard_map/all_to_all | solution.py:167
  71.9 0.9 %shard_map.62 = (bf16[32,16,128]{2,1,0:T(8,128)(2,1)}, bf16[32,16,128]{2,1,0:T(8,128)(2,1)}) custom-call(bf16[256,4,128]{2,1,0:T(4,128)(2,1)S(1)} %all_to_all.11.mine), custom_call_target="tpu_custom_call" | custom-call | tf_op jit(solution)/shard_map/pallas_call | solution.py:19

commit v9 on v8

--- a/solution.py
+++ b/solution.py
@@ -109,11 +109,9 @@
 
 
 def multiply_kernel(left, right, back, held):
-    total = None
-    for core in range(2):
-        lhs = jnp.concatenate([left[(2 * r + core) * 32 : (2 * r + core + 1) * 32, :] for r in range(8)])
-        term = jnp.dot(right[core], lhs, preferred_element_type=jnp.float32)
-        total = term if total is None else total + term
+    blocks = [left[(2 * r + core) * 32 : (2 * r + core + 1) * 32, :] for core in range(2) for r in range(8)]
+    rhs = jnp.concatenate([right[0], right[1]], axis=1)
+    total = jnp.dot(rhs, jnp.concatenate(blocks), preferred_element_type=jnp.float32)
     total = total * FACTOR
     for half in range(2):
         for q in range(4):

time: 73 us -> 73 us (level)
  no operation moved by 1% of the time
where the time goes in v9:
time: 73 us; the launch traced here: 72.8 us
  blocking collectives  68.4 us (94%)
  Pallas kernels  2.6 us (4%)
  other arithmetic  1.13 us (2%)
    all_to_all x1, blocking collectives, body(): lax.all_to_all(pack(out_left, out_right, in_left, in_right), CHIPS, 0, 0,...  41.6 us
    all_to_all x1, blocking collectives, body(): return unpack(lax.all_to_all(back, CHIPS, 0, 0, tiled=True))  24.6 us
    pallas_call x4, Pallas kernels, call(): pl.pallas_call(kernel, out_shape=shape, in_specs=[pl.BlockSpec(memory_spa...  2.6 us
    all_gather x1, blocking collectives, body(): both = lax.all_gather(right, 'core', axis=0, tiled=False)  2.18 us

profile of v9, /device:TPU:8, one launch (start us, length us, event | category | flops | bytes accessed | tf_op | source)
XLA Modules:
  0.0 72.8 jit_solution(15930757098219471815)
XLA Ops:
  0.6 1.1 %pad_maximum_fusion = bf16[2048,128]{1,0:T(8,128)(2,1)S(1)} fusion(bf16[512,128]{1,0:T(8,128)(2,1)} %bitcast.8, bf16[512,128]{1,0:T(8,128)(2,1)} %bitcast.9, bf16[512,128]{1,0:T(8,128)(2,1)} %bitcast.10, bf16[512,128]{1,0:T(8,128)(2,1)} %bitcast.11), kind=kLoop, calls=%fused_computation | loop fusion | flops 2097152 | bytes 1048576 | tf_op jit(solution)/shard_map/concatenate | solution.py:69
  1.8 0.4 shard_map.59
  2.1 41.6 %all_to_all.10.got = bf16[256,8,128]{2,1,0:T(8,128)(2,1)S(1)} all-to-all(bf16[256,8,128]{2,1,0:T(8,128)(2,1)S(1)} %shard_map.59), channel_id=1, replica_groups=mesh['y_lo'=2,'x'=4,'core'=2,'y_hi'=4,'z'=8] {'y_hi','y_lo','z','x'}, dimensions={0} | all-to-all | bytes 1048576 | tf_op jit(solution)/shard_map/all_to_all | solution.py:161
  43.8 0.7 shard_map.60
  44.5 2.2 %all-gather = bf16[1024,256]{1,0:T(8,128)(2,1)S(1)} all-gather(bf16[512,256]{1,0:T(8,128)(2,1)S(1)} %get-tuple-element.5), channel_id=2, replica_groups=mesh['y_lo'=2,'x'=4,'core'=2,'y_hi'=4,'z'=8] {'core'}, dimensions={0}, use_global_device_ids=true | all-gather | bytes 786432 | tf_op jit(solution)/shard_map/all_gather | solution.py:163
  46.7 0.6 shard_map.61
  47.3 24.6 %all_to_all.11.mine = bf16[256,4,128]{2,1,0:T(4,128)(2,1)S(1)} all-to-all(bf16[256,4,128]{2,1,0:T(4,128)(2,1)S(1)} %shard_map.61), channel_id=1, replica_groups=mesh['y_lo'=2,'x'=4,'core'=2,'y_hi'=4,'z'=8] {'y_hi','y_lo','z','x'}, dimensions={0} | all-to-all | bytes 524288 | tf_op jit(solution)/shard_map/all_to_all | solution.py:165
  71.9 0.9 %shard_map.62 = (bf16[32,16,128]{2,1,0:T(8,128)(2,1)}, bf16[32,16,128]{2,1,0:T(8,128)(2,1)}) custom-call(bf16[256,4,128]{2,1,0:T(4,128)(2,1)S(1)} %all_to_all.11.mine), custom_call_target="tpu_custom_call" | custom-call | tf_op jit(solution)/shard_map/pallas_call | solution.py:19
